TPU v7x, 32 devices: a whole 2x2x4 slice. The times are simulated.
32 devices in a mesh: box: 16 (over z, y, x), samp: 2 (over core).
Axes of the slice: x: 2, y: 2, z: 4, core: 2. Of those that a mesh axis runs over, the one named last changes fastest.
Arguments:
- currents: bfloat16 [128, 8, 128], P(('box', 'samp')), may hold values from -6 to 6
- radiation: bfloat16 [128, 2, 2, 512, 128], P(('box', 'samp')), may hold values from -0.1875 to 0.1875
- near_blocks: bfloat16 [128, 8, 2, 128, 128], P(('box', 'samp')), may hold values from -0.125 to 0.125
- near_src: int32 [128, 8], P(('box', 'samp')), may hold values from 0 to 127, as said below
- leaf_parent: int32 [128], P('box'), may hold values from 0 to 255, as said below
- leaf_shift: int32 [128], P('box'), may hold values from 0 to 7
- shift_table: bfloat16 [8, 2, 8192], P(None, None, 'samp'), may hold values from -4 to 4
- interp_idx: int32 [64, 2], P('samp'), may hold values from 0 to 3, as said below
- interp_val: bfloat16 [64, 2, 128, 128], P('samp'), may hold values from -0.375 to 0.375
- top_src: int32 [256, 16], P('box'), may hold values from 0 to 255, as said below
- top_disp: int32 [256, 16], P('box'), may hold values from 0 to 31
- trans_table: bfloat16 [32, 2, 8192], P(None, None, 'samp'), may hold values from -1 to 1
Outputs:
- matvec: float32 [128, 8, 128], P(('box', 'samp'))
Inputs may be any that keep to these rules, and one draw needn't show every extreme that they name: `near_src`: entry 0 of a leaf's row is the leaf itself; every entry lies in the 4 leaves of the leaf's own device or of the devices just before and after it in box+samp order (leaves numbered box-major), and these ends are reached. `leaf_parent`: the parent of leaf l lies in its box group: its value divided by 16 equals l divided by 8. `interp_idx`: the 2 entries of a row differ. `top_src`: a source of top box t is another box of t's group (t // 16), or one of the last 8 boxes of the group before it, or one of the first 8 boxes of the group after it; both rims are reached.
All inputs are finite; a program needn't handle non-finite values.
Results may differ from a plain program's by a relative error of at most 0.013.
Values may be sent and summed in bfloat16 or wider, within the bound.
No kernel may reach another device: no remote copies, remote signals or barrier semaphores. Data moves between devices by JAX's collectives and lax.ppermute only.
A program may use at most 64 MiB of HBM per device.

v0:
```python
import jax
import jax.numpy as jnp
from jax import lax
from jax.sharding import PartitionSpec as P

HIGHEST = lax.Precision.HIGHEST


def with_halo(cells, sides, width):
    for axis, dim in sides:
        count = lax.axis_size(axis)
        ends = count - 1
        head = lax.slice_in_dim(cells, 0, width, axis=dim)
        tail = lax.slice_in_dim(cells, cells.shape[dim] - width, cells.shape[dim], axis=dim)
        cells = jnp.concatenate(
            [
                lax.ppermute(tail, axis, [(i, (i + 1) % count) for i in range(ends)]),
                cells,
                lax.ppermute(head, axis, [((i + 1) % count, i) for i in range(ends)]),
            ],
            axis=dim,
        )
    return cells


def complex_mul(a_real, a_imag, b_real, b_imag):
    return (a_real * b_real - a_imag * b_imag, a_real * b_imag + a_imag * b_real)


def contract(form, first_op, second_op):
    return jnp.einsum(form, first_op, second_op, preferred_element_type=jnp.float32)


def per_device(
    currents,
    radiation,
    near_blocks,
    near_src,
    leaf_parent,
    leaf_shift,
    shift_table,
    interp_idx,
    interp_val,
    top_src,
    top_disp,
    trans_table,
):
    leaf_count = currents.shape[0]
    half_comp = currents.shape[1]
    excite = half_comp // 2
    comps = 2 * half_comp
    samp_count = lax.axis_size("samp")
    group_index = lax.axis_index("box")
    first_leaf = (group_index * samp_count + lax.axis_index("samp")) * leaf_count
    top_count = top_src.shape[0]
    block_size = interp_val.shape[2]
    leaf_samples = radiation.shape[3]
    in_blocks = leaf_samples // block_size
    local_blocks = interp_val.shape[0]
    local_samples = local_blocks * block_size
    neighbours = with_halo(currents, ((("box", "samp"), 0),), leaf_count)
    rad_real = radiation[:, :, 0]
    rad_imag = radiation[:, :, 1]
    form_out = "lpqu,leu->lpeq"
    out_real = contract(form_out, rad_real, currents[:, :excite]) - contract(
        form_out, rad_imag, currents[:, excite:]
    )
    out_imag = contract(form_out, rad_real, currents[:, excite:]) + contract(
        form_out, rad_imag, currents[:, :excite]
    )
    patterns = jnp.concatenate(
        [
            out_real.reshape(leaf_count, half_comp, leaf_samples),
            out_imag.reshape(leaf_count, half_comp, leaf_samples),
        ],
        axis=1,
    ).astype(jnp.bfloat16)
    piece = lax.all_gather(patterns, "samp", axis=0, tiled=True)
    piece_rows = piece.shape[0]
    picked = piece.reshape(piece_rows, comps, in_blocks, block_size)[:, :, interp_idx, :]
    moved_rows = contract("lcbri,brki->lcbk", picked, interp_val)
    moved = moved_rows.reshape(piece_rows, comps, local_samples)
    shift_onehot = (leaf_shift[:, None] == jnp.arange(shift_table.shape[0])[None, :]).astype(
        jnp.bfloat16
    )
    shift_rows = contract("ln,nrk->lrk", shift_onehot, shift_table)
    shift_real = shift_rows[:, 0:1]
    shift_imag = shift_rows[:, 1:2]
    up_real, up_imag = complex_mul(
        moved[:, :half_comp], moved[:, half_comp:], shift_real, shift_imag
    )
    shifted = jnp.concatenate([up_real, up_imag], axis=1)
    parent_local = leaf_parent - group_index * top_count
    member = parent_local[None, :] == jnp.arange(top_count)[:, None]
    top_patterns = jnp.einsum(
        "tl,lck->tck", member.astype(jnp.float32), shifted, precision=HIGHEST
    ).astype(jnp.bfloat16)
    rim_width = top_count // 2
    padded = with_halo(top_patterns, (("box", 0),), rim_width)
    base_index = group_index * top_count - rim_width
    disp_count = trans_table.shape[0]

    def add_entry(entry, total):
        source_rows = jnp.take(padded, top_src[:, entry] - base_index, axis=0).astype(jnp.float32)
        disp_onehot = (top_disp[:, entry][:, None] == jnp.arange(disp_count)[None, :]).astype(
            jnp.bfloat16
        )
        coeff = contract("tn,nrk->trk", disp_onehot, trans_table)
        part_real, part_imag = complex_mul(
            coeff[:, 0:1], coeff[:, 1:2], source_rows[:, :half_comp], source_rows[:, half_comp:]
        )
        return total + jnp.concatenate([part_real, part_imag], axis=1)

    incoming = lax.fori_loop(
        0, top_src.shape[1], add_entry, jnp.zeros((top_count, comps, local_samples), jnp.float32)
    ).astype(jnp.bfloat16)
    spread = contract("tl,tck->lck", member.astype(jnp.bfloat16), incoming)
    down_real, down_imag = complex_mul(
        shift_real, -shift_imag, spread[:, :half_comp], spread[:, half_comp:]
    )
    down = jnp.concatenate([down_real, down_imag], axis=1).astype(jnp.bfloat16)
    block_onehot = (interp_idx[:, :, None] == jnp.arange(in_blocks)[None, None, :]).astype(
        jnp.float32
    )
    parts = contract(
        "lcbk,brki->lcbri",
        down.reshape(leaf_count * lax.axis_size("samp"), comps, local_blocks, block_size),
        interp_val,
    )
    folded = jnp.einsum("lcbri,brq->lcqi", parts, block_onehot, precision=HIGHEST)
    far = lax.psum_scatter(
        folded.reshape(leaf_count * lax.axis_size("samp"), comps, leaf_samples).astype(
            jnp.bfloat16
        ),
        "samp",
        scatter_dimension=0,
        tiled=True,
    )
    far_real = far[:, :half_comp].reshape(leaf_count, 2, excite, leaf_samples)
    far_imag = far[:, half_comp:].reshape(leaf_count, 2, excite, leaf_samples)
    form_back = "lpqu,lpeq->leu"
    recv_real = contract(form_back, rad_real, far_real) + contract(form_back, rad_imag, far_imag)
    recv_imag = contract(form_back, rad_real, far_imag) - contract(form_back, rad_imag, far_real)
    near_rows = jnp.take(neighbours, near_src - first_leaf + leaf_count, axis=0)
    block_real = near_blocks[:, :, 0]
    block_imag = near_blocks[:, :, 1]
    form_near = "lnuv,lnev->leu"
    near_real = contract(form_near, block_real, near_rows[:, :, :excite]) - contract(
        form_near, block_imag, near_rows[:, :, excite:]
    )
    near_imag = contract(form_near, block_real, near_rows[:, :, excite:]) + contract(
        form_near, block_imag, near_rows[:, :, :excite]
    )
    return jnp.concatenate([recv_real + near_real, recv_imag + near_imag], axis=1)


def solution(mesh):
    placed = (
        P(("box", "samp"), None, None),
        P(("box", "samp"), None, None, None, None),
        P(("box", "samp"), None, None, None, None),
        P(("box", "samp"), None),
        P("box"),
        P("box"),
        P(None, None, "samp"),
        P("samp", None),
        P("samp", None, None, None),
        P("box", None),
        P("box", None),
        P(None, None, "samp"),
    )
    return jax.shard_map(
        per_device,
        mesh=mesh,
        in_specs=placed,
        out_specs=P(("box", "samp"), None, None),
        check_vma=False,
    )
```

profile of v0, /device:TPU:0, one launch (start us, length us, event | category | flops | bytes accessed | tf_op | source)
XLA Modules:
  0.0 373.9 jit_solution(5036672421281757423)
XLA Ops:
  30.6 5.7 %collective-permute-start = (bf16[8,16,4096]{2,0,1:T(8,128)(2,1)}, bf16[8,16,4096]{2,0,1:T(8,128)(2,1)}, u32[]{:S(2)}, u32[]{:S(2)}) collective-permute-start(bf16[8,16,4096]{2,0,1:T(8,128)(2,1)} %get-tuple-element.208), channel_id=1, source_target_pairs={{0,2},{2,4},{4,6},{6,8},{8,10},{10,12},{12,14},{14,16},{16,18},{18... | collective-permute-start | bytes 3145736 | tf_op jit(solution)/shard_map/ppermute | solution.py:17
  45.5 35.5 %collective-permute-done = bf16[8,16,4096]{2,0,1:T(8,128)(2,1)} collective-permute-done((bf16[8,16,4096]{2,0,1:T(8,128)(2,1)}, bf16[8,16,4096]{2,0,1:T(8,128)(2,1)}, u32[]{:S(2)}, u32[]{:S(2)}) %collective-permute-start) | collective-permute-done | bytes 1048608 | tf_op jit(solution)/shard_map/ppermute | solution.py:17
  89.5 250.2 %while.14 = (s32[]{:T(128)}, f32[16,16,4096]{2,1,0:T(8,128)}, s32[16,16]{0,1:T(8,128)S(1)}, bf16[32,2,4096]{2,0,1:T(8,128)(2,1)S(1)}, s32[16,16]{0,1:T(8,128)S(1...) while((s32[]{:T(128)}, f32[16,16,4096]{2,1,0:T(8,128)}, ...), condition=%wide.region_1.0_spmd.clone, body=%wide.region_0.1_spmd.clone.sunk | while | flops 16778868 | bytes 34083408 | solution.py:114
  89.5 4.3 %gather_fusion = bf16[16,16,4096]{2,1,0:T(8,128)(2,1)} fusion(bf16[32,16,4096]{2,1,0:T(8,128)(2,1)} %get-tuple-element.294, s32[1024]{0:T(1024)S(1)} %pad_clamp_fusion.4), kind=kCustom, calls=%fused_computation.clone.clone.1 | custom fusion | bytes 4194368 | tf_op jit(solution)/shard_map/while/body/eval_jaxpr/jit(_take)/gather | solution.py:104
  98.7 5.2 %maximum_add_fusion.2 = f32[16,16,4096]{2,1,0:T(8,128)} fusion(f32[16,8,4096]{2,1,0:T(8,128)} %get-tuple-element.268, f32[16,8,4096]{2,1,0:T(8,128)} %get-tuple-element.269, f32[16,16,4096]{2,1,0:T(8,128)} %get-tuple-element.280, pred[]{:T(512)S(6)} %compare.3), kind=kLoop, calls=%fused_computation.3.clone.1 | loop fusion | flops 3145728 | bytes 12582913 | tf_op jit(solution)/shard_map/while/body/eval_jaxpr/add | solution.py:112
  104.0 4.3 %gather_fusion = bf16[16,16,4096]{2,1,0:T(8,128)(2,1)} fusion(bf16[32,16,4096]{2,1,0:T(8,128)(2,1)} %get-tuple-element.294, s32[1024]{0:T(1024)S(1)} %pad_clamp_fusion.4), kind=kCustom, calls=%fused_computation.clone.clone.1 | custom fusion | bytes 4194368 | tf_op jit(solution)/shard_map/while/body/eval_jaxpr/jit(_take)/gather | solution.py:104
  113.2 6.5 %maximum_add_fusion.2 = f32[16,16,4096]{2,1,0:T(8,128)} fusion(f32[16,8,4096]{2,1,0:T(8,128)} %get-tuple-element.268, f32[16,8,4096]{2,1,0:T(8,128)} %get-tuple-element.269, f32[16,16,4096]{2,1,0:T(8,128)} %get-tuple-element.280, pred[]{:T(512)S(6)} %compare.3), kind=kLoop, calls=%fused_computation.3.clone.1 | loop fusion | flops 3145728 | bytes 12582913 | tf_op jit(solution)/shard_map/while/body/eval_jaxpr/add | solution.py:112
  128.9 6.5 %maximum_add_fusion.2 = f32[16,16,4096]{2,1,0:T(8,128)} fusion(f32[16,8,4096]{2,1,0:T(8,128)} %get-tuple-element.268, f32[16,8,4096]{2,1,0:T(8,128)} %get-tuple-element.269, f32[16,16,4096]{2,1,0:T(8,128)} %get-tuple-element.280, pred[]{:T(512)S(6)} %compare.3), kind=kLoop, calls=%fused_computation.3.clone.1 | loop fusion | flops 3145728 | bytes 12582913 | tf_op jit(solution)/shard_map/while/body/eval_jaxpr/add | solution.py:112
  135.4 4.3 %gather_fusion = bf16[16,16,4096]{2,1,0:T(8,128)(2,1)} fusion(bf16[32,16,4096]{2,1,0:T(8,128)(2,1)} %get-tuple-element.294, s32[1024]{0:T(1024)S(1)} %pad_clamp_fusion.4), kind=kCustom, calls=%fused_computation.clone.clone.1 | custom fusion | bytes 4194368 | tf_op jit(solution)/shard_map/while/body/eval_jaxpr/jit(_take)/gather | solution.py:104
  144.6 6.5 %maximum_add_fusion.2 = f32[16,16,4096]{2,1,0:T(8,128)} fusion(f32[16,8,4096]{2,1,0:T(8,128)} %get-tuple-element.268, f32[16,8,4096]{2,1,0:T(8,128)} %get-tuple-element.269, f32[16,16,4096]{2,1,0:T(8,128)} %get-tuple-element.280, pred[]{:T(512)S(6)} %compare.3), kind=kLoop, calls=%fused_computation.3.clone.1 | loop fusion | flops 3145728 | bytes 12582913 | tf_op jit(solution)/shard_map/while/body/eval_jaxpr/add | solution.py:112
  151.1 4.3 %gather_fusion = bf16[16,16,4096]{2,1,0:T(8,128)(2,1)} fusion(bf16[32,16,4096]{2,1,0:T(8,128)(2,1)} %get-tuple-element.294, s32[1024]{0:T(1024)S(1)} %pad_clamp_fusion.4), kind=kCustom, calls=%fused_computation.clone.clone.1 | custom fusion | bytes 4194368 | tf_op jit(solution)/shard_map/while/body/eval_jaxpr/jit(_take)/gather | solution.py:104
  160.3 6.5 %maximum_add_fusion.2 = f32[16,16,4096]{2,1,0:T(8,128)} fusion(f32[16,8,4096]{2,1,0:T(8,128)} %get-tuple-element.268, f32[16,8,4096]{2,1,0:T(8,128)} %get-tuple-element.269, f32[16,16,4096]{2,1,0:T(8,128)} %get-tuple-element.280, pred[]{:T(512)S(6)} %compare.3), kind=kLoop, calls=%fused_computation.3.clone.1 | loop fusion | flops 3145728 | bytes 12582913 | tf_op jit(solution)/shard_map/while/body/eval_jaxpr/add | solution.py:112
  176.0 6.5 %maximum_add_fusion.2 = f32[16,16,4096]{2,1,0:T(8,128)} fusion(f32[16,8,4096]{2,1,0:T(8,128)} %get-tuple-element.268, f32[16,8,4096]{2,1,0:T(8,128)} %get-tuple-element.269, f32[16,16,4096]{2,1,0:T(8,128)} %get-tuple-element.280, pred[]{:T(512)S(6)} %compare.3), kind=kLoop, calls=%fused_computation.3.clone.1 | loop fusion | flops 3145728 | bytes 12582913 | tf_op jit(solution)/shard_map/while/body/eval_jaxpr/add | solution.py:112
  182.5 4.3 %gather_fusion = bf16[16,16,4096]{2,1,0:T(8,128)(2,1)} fusion(bf16[32,16,4096]{2,1,0:T(8,128)(2,1)} %get-tuple-element.294, s32[1024]{0:T(1024)S(1)} %pad_clamp_fusion.4), kind=kCustom, calls=%fused_computation.clone.clone.1 | custom fusion | bytes 4194368 | tf_op jit(solution)/shard_map/while/body/eval_jaxpr/jit(_take)/gather | solution.py:104
  191.7 6.5 %maximum_add_fusion.2 = f32[16,16,4096]{2,1,0:T(8,128)} fusion(f32[16,8,4096]{2,1,0:T(8,128)} %get-tuple-element.268, f32[16,8,4096]{2,1,0:T(8,128)} %get-tuple-element.269, f32[16,16,4096]{2,1,0:T(8,128)} %get-tuple-element.280, pred[]{:T(512)S(6)} %compare.3), kind=kLoop, calls=%fused_computation.3.clone.1 | loop fusion | flops 3145728 | bytes 12582913 | tf_op jit(solution)/shard_map/while/body/eval_jaxpr/add | solution.py:112
  207.4 6.5 %maximum_add_fusion.2 = f32[16,16,4096]{2,1,0:T(8,128)} fusion(f32[16,8,4096]{2,1,0:T(8,128)} %get-tuple-element.268, f32[16,8,4096]{2,1,0:T(8,128)} %get-tuple-element.269, f32[16,16,4096]{2,1,0:T(8,128)} %get-tuple-element.280, pred[]{:T(512)S(6)} %compare.3), kind=kLoop, calls=%fused_computation.3.clone.1 | loop fusion | flops 3145728 | bytes 12582913 | tf_op jit(solution)/shard_map/while/body/eval_jaxpr/add | solution.py:112
  213.9 4.3 %gather_fusion = bf16[16,16,4096]{2,1,0:T(8,128)(2,1)} fusion(bf16[32,16,4096]{2,1,0:T(8,128)(2,1)} %get-tuple-element.294, s32[1024]{0:T(1024)S(1)} %pad_clamp_fusion.4), kind=kCustom, calls=%fused_computation.clone.clone.1 | custom fusion | bytes 4194368 | tf_op jit(solution)/shard_map/while/body/eval_jaxpr/jit(_take)/gather | solution.py:104
  223.1 6.5 %maximum_add_fusion.2 = f32[16,16,4096]{2,1,0:T(8,128)} fusion(f32[16,8,4096]{2,1,0:T(8,128)} %get-tuple-element.268, f32[16,8,4096]{2,1,0:T(8,128)} %get-tuple-element.269, f32[16,16,4096]{2,1,0:T(8,128)} %get-tuple-element.280, pred[]{:T(512)S(6)} %compare.3), kind=kLoop, calls=%fused_computation.3.clone.1 | loop fusion | flops 3145728 | bytes 12582913 | tf_op jit(solution)/shard_map/while/body/eval_jaxpr/add | solution.py:112
  229.7 4.3 %gather_fusion = bf16[16,16,4096]{2,1,0:T(8,128)(2,1)} fusion(bf16[32,16,4096]{2,1,0:T(8,128)(2,1)} %get-tuple-element.294, s32[1024]{0:T(1024)S(1)} %pad_clamp_fusion.4), kind=kCustom, calls=%fused_computation.clone.clone.1 | custom fusion | bytes 4194368 | tf_op jit(solution)/shard_map/while/body/eval_jaxpr/jit(_take)/gather | solution.py:104
  238.9 6.5 %maximum_add_fusion.2 = f32[16,16,4096]{2,1,0:T(8,128)} fusion(f32[16,8,4096]{2,1,0:T(8,128)} %get-tuple-element.268, f32[16,8,4096]{2,1,0:T(8,128)} %get-tuple-element.269, f32[16,16,4096]{2,1,0:T(8,128)} %get-tuple-element.280, pred[]{:T(512)S(6)} %compare.3), kind=kLoop, calls=%fused_computation.3.clone.1 | loop fusion | flops 3145728 | bytes 12582913 | tf_op jit(solution)/shard_map/while/body/eval_jaxpr/add | solution.py:112
  245.4 4.3 %gather_fusion = bf16[16,16,4096]{2,1,0:T(8,128)(2,1)} fusion(bf16[32,16,4096]{2,1,0:T(8,128)(2,1)} %get-tuple-element.294, s32[1024]{0:T(1024)S(1)} %pad_clamp_fusion.4), kind=kCustom, calls=%fused_computation.clone.clone.1 | custom fusion | bytes 4194368 | tf_op jit(solution)/shard_map/while/body/eval_jaxpr/jit(_take)/gather | solution.py:104
  254.6 6.5 %maximum_add_fusion.2 = f32[16,16,4096]{2,1,0:T(8,128)} fusion(f32[16,8,4096]{2,1,0:T(8,128)} %get-tuple-element.268, f32[16,8,4096]{2,1,0:T(8,128)} %get-tuple-element.269, f32[16,16,4096]{2,1,0:T(8,128)} %get-tuple-element.280, pred[]{:T(512)S(6)} %compare.3), kind=kLoop, calls=%fused_computation.3.clone.1 | loop fusion | flops 3145728 | bytes 12582913 | tf_op jit(solution)/shard_map/while/body/eval_jaxpr/add | solution.py:112
  261.1 4.3 %gather_fusion = bf16[16,16,4096]{2,1,0:T(8,128)(2,1)} fusion(bf16[32,16,4096]{2,1,0:T(8,128)(2,1)} %get-tuple-element.294, s32[1024]{0:T(1024)S(1)} %pad_clamp_fusion.4), kind=kCustom, calls=%fused_computation.clone.clone.1 | custom fusion | bytes 4194368 | tf_op jit(solution)/shard_map/while/body/eval_jaxpr/jit(_take)/gather | solution.py:104
  270.3 6.5 %maximum_add_fusion.2 = f32[16,16,4096]{2,1,0:T(8,128)} fusion(f32[16,8,4096]{2,1,0:T(8,128)} %get-tuple-element.268, f32[16,8,4096]{2,1,0:T(8,128)} %get-tuple-element.269, f32[16,16,4096]{2,1,0:T(8,128)} %get-tuple-element.280, pred[]{:T(512)S(6)} %compare.3), kind=kLoop, calls=%fused_computation.3.clone.1 | loop fusion | flops 3145728 | bytes 12582913 | tf_op jit(solution)/shard_map/while/body/eval_jaxpr/add | solution.py:112
  286.0 6.5 %maximum_add_fusion.2 = f32[16,16,4096]{2,1,0:T(8,128)} fusion(f32[16,8,4096]{2,1,0:T(8,128)} %get-tuple-element.268, f32[16,8,4096]{2,1,0:T(8,128)} %get-tuple-element.269, f32[16,16,4096]{2,1,0:T(8,128)} %get-tuple-element.280, pred[]{:T(512)S(6)} %compare.3), kind=kLoop, calls=%fused_computation.3.clone.1 | loop fusion | flops 3145728 | bytes 12582913 | tf_op jit(solution)/shard_map/while/body/eval_jaxpr/add | solution.py:112
  292.5 4.3 %gather_fusion = bf16[16,16,4096]{2,1,0:T(8,128)(2,1)} fusion(bf16[32,16,4096]{2,1,0:T(8,128)(2,1)} %get-tuple-element.294, s32[1024]{0:T(1024)S(1)} %pad_clamp_fusion.4), kind=kCustom, calls=%fused_computation.clone.clone.1 | custom fusion | bytes 4194368 | tf_op jit(solution)/shard_map/while/body/eval_jaxpr/jit(_take)/gather | solution.py:104
  301.7 6.5 %maximum_add_fusion.2 = f32[16,16,4096]{2,1,0:T(8,128)} fusion(f32[16,8,4096]{2,1,0:T(8,128)} %get-tuple-element.268, f32[16,8,4096]{2,1,0:T(8,128)} %get-tuple-element.269, f32[16,16,4096]{2,1,0:T(8,128)} %get-tuple-element.280, pred[]{:T(512)S(6)} %compare.3), kind=kLoop, calls=%fused_computation.3.clone.1 | loop fusion | flops 3145728 | bytes 12582913 | tf_op jit(solution)/shard_map/while/body/eval_jaxpr/add | solution.py:112
  308.2 4.3 %gather_fusion = bf16[16,16,4096]{2,1,0:T(8,128)(2,1)} fusion(bf16[32,16,4096]{2,1,0:T(8,128)(2,1)} %get-tuple-element.294, s32[1024]{0:T(1024)S(1)} %pad_clamp_fusion.4), kind=kCustom, calls=%fused_computation.clone.clone.1 | custom fusion | bytes 4194368 | tf_op jit(solution)/shard_map/while/body/eval_jaxpr/jit(_take)/gather | solution.py:104
  317.4 6.5 %maximum_add_fusion.2 = f32[16,16,4096]{2,1,0:T(8,128)} fusion(f32[16,8,4096]{2,1,0:T(8,128)} %get-tuple-element.268, f32[16,8,4096]{2,1,0:T(8,128)} %get-tuple-element.269, f32[16,16,4096]{2,1,0:T(8,128)} %get-tuple-element.280, pred[]{:T(512)S(6)} %compare.3), kind=kLoop, calls=%fused_computation.3.clone.1 | loop fusion | flops 3145728 | bytes 12582913 | tf_op jit(solution)/shard_map/while/body/eval_jaxpr/add | solution.py:112
  323.9 4.3 %gather_fusion = bf16[16,16,4096]{2,1,0:T(8,128)(2,1)} fusion(bf16[32,16,4096]{2,1,0:T(8,128)(2,1)} %get-tuple-element.294, s32[1024]{0:T(1024)S(1)} %pad_clamp_fusion.4), kind=kCustom, calls=%fused_computation.clone.clone.1 | custom fusion | bytes 4194368 | tf_op jit(solution)/shard_map/while/body/eval_jaxpr/jit(_take)/gather | solution.py:104
  333.1 6.5 %maximum_add_fusion.2 = f32[16,16,4096]{2,1,0:T(8,128)} fusion(f32[16,8,4096]{2,1,0:T(8,128)} %get-tuple-element.268, f32[16,8,4096]{2,1,0:T(8,128)} %get-tuple-element.269, f32[16,16,4096]{2,1,0:T(8,128)} %get-tuple-element.280, pred[]{:T(512)S(6)} %compare.3), kind=kLoop, calls=%fused_computation.3.clone.1 | loop fusion | flops 3145728 | bytes 12582913 | tf_op jit(solution)/shard_map/while/body/eval_jaxpr/add | solution.py:112
  353.4 5.3 %reduce-scatter.2.cloned.1.call-done = bf16[4,16,512]{2,1,0:T(8,128)(2,1)} async-done(((bf16[8,16,512]{2,1,0:T(8,128)(2,1)}), bf16[4,16,512]{2,1,0:T(8,128)(2,1)}) %reduce-scatter.2.cloned.1.call-update) | async-done | bytes 65552 | tf_op jit(solution)/shard_map/reduce_scatter | solution.py:131
  (205 shorter events, 159.6 us)
Async XLA Ops:
  6.5 10.4 %copy-start = (bf16[32,2,128,128]{3,2,1,0:T(8,128)(2,1)S(1)}, bf16[32,2,128,128]{3,2,1,0:T(8,128)(2,1)}, u32[]{:S(2)}) copy-start(bf16[32,2,128,128]{3,2,1,0:T(8,128)(2,1)} %param.22) | copy-start | bytes 6291460
  6.5 3.8 %copy-start.6 = (bf16[4,8,128]{2,1,0:T(8,128)(2,1)S(1)}, bf16[4,8,128]{2,1,0:T(8,128)(2,1)}, u32[]{:S(2)}) copy-start(bf16[4,8,128]{2,1,0:T(8,128)(2,1)} %param.14) | copy-start | bytes 24580
  6.5 3.5 copy-start.12
  6.5 3.5 copy-start.7
  6.5 352.2 %reduce-scatter.2.cloned.1.call-start = ((), (), s32[]{:S(2)}) async-start(), calls=%async_computation.1 | async-start | bytes 196608 | tf_op jit(solution)/shard_map/reduce_scatter | solution.py:131
  6.6 3.7 %copy-start.1 = (bf16[4,2,2,512,128]{4,3,2,1,0:T(8,128)(2,1)S(1)}, bf16[4,2,2,512,128]{4,3,2,1,0:T(8,128)(2,1)}, u32[]{:S(2)}) copy-start(bf16[4,2,2,512,128]{4,3,2,1,0:T(8,128)(2,1)} %param.15) | copy-start | bytes 6291460
  10.0 4.4 %copy-start.10 = (s32[32,2]{0,1:T(2,128)S(1)}, s32[32,2]{0,1:T(2,128)}, u32[]{:S(2)}) copy-start(s32[32,2]{0,1:T(2,128)} %param.21) | copy-start | bytes 772
  21.8 2.7 copy-start.13
  28.6 2.0 copy-start.3
  28.6 12.1 %copy-start.11 = (s32[4,8]{1,0:T(4,128)S(1)}, s32[4,8]{1,0:T(4,128)}, u32[]{:S(2)}) copy-start(s32[4,8]{1,0:T(4,128)} %param.17) | copy-start | bytes 388
  28.6 12.2 %copy-start.5 = (bf16[32,2,4096]{2,1,0:T(2,128)(2,1)S(1)}, bf16[32,2,4096]{2,1,0:T(2,128)(2,1)}, u32[]{:S(2)}) copy-start(bf16[32,2,4096]{2,1,0:T(2,128)(2,1)} %param.25) | copy-start | bytes 1572868
  28.6 12.5 %copy-start.8 = (s32[16,16]{1,0:T(8,128)S(1)}, s32[16,16]{1,0:T(8,128)}, u32[]{:S(2)}) copy-start(s32[16,16]{1,0:T(8,128)} %param.24) | copy-start | bytes 3076
  28.6 12.6 %copy-start.9 = (s32[16,16]{1,0:T(8,128)S(1)}, s32[16,16]{1,0:T(8,128)}, u32[]{:S(2)}) copy-start(s32[16,16]{1,0:T(8,128)} %param.23) | copy-start | bytes 3076
  30.6 50.4 %collective-permute-start = (bf16[8,16,4096]{2,0,1:T(8,128)(2,1)}, bf16[8,16,4096]{2,0,1:T(8,128)(2,1)}, u32[]{:S(2)}, u32[]{:S(2)}) collective-permute-start(bf16[8,16,4096]{2,0,1:T(8,128)(2,1)} %get-tuple-element.208), channel_id=1, source_target_pairs={{0,2},{2,4},{4,6},{6,8},{8,10},{10,12},{12,14},{14,16},{16,18},{18... | collective-permute-start | bytes 3145736 | tf_op jit(solution)/shard_map/ppermute | solution.py:17
  36.3 46.6 %collective-permute-start.1 = (bf16[8,16,4096]{2,0,1:T(8,128)(2,1)}, bf16[8,16,4096]{2,0,1:T(8,128)(2,1)}, u32[]{:S(2)}, u32[]{:S(2)}) collective-permute-start(bf16[8,16,4096]{2,0,1:T(8,128)(2,1)} %get-tuple-element.209), channel_id=1, source_target_pairs={{2,0},{4,2},{6,4},{8,6},{10,8},{12,10},{14,12},{16,14},{18,16},{20... | collective-permute-start | bytes 3145736 | tf_op jit(solution)/shard_map/ppermute | solution.py:19
  37.6 3.7 collective-permute-start.2
  39.4 5.5 %collective-permute-start.3 = (bf16[4,8,128]{2,1,0:T(8,128)(2,1)S(1)}, bf16[4,8,128]{2,1,0:T(8,128)(2,1)S(1)}, u32[]{:S(2)}, u32[]{:S(2)}) collective-permute-start(bf16[4,8,128]{2,1,0:T(8,128)(2,1)S(1)} %copy-done.6), channel_id=1, source_target_pairs={{1,0},{2,1},{3,2},{4,3},{5,4},{6,5},{7,6},{8,7},{9,8},{10,9},{11,1... | collective-permute-start | bytes 24584 | tf_op jit(solution)/shard_map/ppermute | solution.py:19
  361.0 3.1 copy-start.2
  361.0 5.0 %copy-start.4 = (bf16[4,8,2,128,128]{4,3,2,1,0:T(8,128)(2,1)S(1)}, bf16[4,8,2,128,128]{4,3,2,1,0:T(8,128)(2,1)}, u32[]{:S(2)}) copy-start(bf16[4,8,2,128,128]{4,3,2,1,0:T(8,128)(2,1)} %param.16) | copy-start | bytes 6291460
Sparse Core Ops, SparseCore 0:
  350.3 8.3 reduce-scatter.1
where the time goes:
time: 376 us; the launch traced here: 374 us
  other arithmetic  184 us (49%)
  local copies, waits for them, and re-layouts  85.7 us (23%)
  waiting for transfers between devices  46.2 us (12%)
  matrix products  31.7 us (8%)
  between operations  13.7 us (4%)
  starting transfers between devices  10.1 us (3%)
    add x16, other arithmetic, add_entry(): return total + jnp.concatenate([part_real, part_imag], axis=1)  102 us
    gather x16, local copies, waits for them, and re-layouts, add_entry(): jnp.take(padded, top_src[:, entry] - base_index, axis=0).astype(jnp.float32)  68.1 us
    sub x17, other arithmetic, complex_mul(): a_real * b_real - a_imag * b_imag  44.5 us
    ppermute x2, waiting for transfers between devices, with_halo(): lax.ppermute(tail, axis, [(i, (i + 1) % count) for i in range(ends)])  35.5 us
    convert_element_type x16, other arithmetic, add_entry(): jnp.take(padded, top_src[:, entry] - base_index, axis=0).astype(jnp.float32)  30.9 us
    dot_general x32, matrix products, contract(): jnp.einsum(form, first_op, second_op, preferred_element_type=jnp.float32)  25.4 us
  transfers between devices with their start and end apart: 5, of which 4 were waited for; matrix products, arithmetic and copies ran while one was open for 1% of the time, Pallas kernels for 0%

commit v1 on v0

v1 whole, which is shorter than its diff:
```python
import functools

import jax
import jax.numpy as jnp
from jax import lax
from jax.experimental import pallas as pl
from jax.experimental.pallas import tpu as pltpu
from jax.sharding import PartitionSpec as P

F32 = jnp.float32
BF16 = jnp.bfloat16
ANY = pl.BlockSpec(memory_space=pl.ANY)
VMEM = pl.BlockSpec(memory_space=pltpu.VMEM)
SMEM = pl.BlockSpec(memory_space=pltpu.SMEM)
NT = (((1,), (1,)), ((), ()))
LIMIT = 48 * 1024 * 1024


def params():
    return pltpu.CompilerParams(vmem_limit_bytes=LIMIT)


def radiate_kernel(cur_ref, meta_ref, rad_hbm, msg_ref, rad_ref, sem):
    leaf_count, in_blocks = cur_ref.shape[0], msg_ref.shape[0]
    block = msg_ref.shape[2]
    half = cur_ref.shape[1] // 2
    copies = [
        pltpu.make_async_copy(rad_hbm.at[leaf], rad_ref.at[leaf], sem.at[leaf])
        for leaf in range(leaf_count)
    ]
    for copy in copies:
        copy.start()
    base = leaf_count * 4 * half
    meta = meta_ref[...]
    zero = jnp.zeros((half, cur_ref.shape[2]), F32)
    left = []
    for leaf in range(leaf_count):
        cur = cur_ref[leaf].astype(F32)
        real, imag = cur[:half], cur[half:]
        pieces = [
            jnp.concatenate(rows, axis=0).astype(BF16)
            for rows in (
                (real, zero, imag, zero),
                (-imag, zero, real, zero),
                (zero, real, zero, imag),
                (zero, -imag, zero, real),
            )
        ]
        left.append(jnp.concatenate(pieces, axis=1))
        row = base + leaf // in_blocks * 4 * half
        msg_ref[leaf % in_blocks, row : row + 4 * half, :] = jnp.concatenate(
            [cur, meta], axis=0
        ).astype(BF16)
    for leaf in range(leaf_count):
        copies[leaf].wait()
        right = jnp.concatenate(
            [rad_ref[leaf, p, r] for p in range(2) for r in range(2)], axis=1
        )
        out = lax.dot_general(left[leaf], right, NT, preferred_element_type=F32).astype(BF16)
        for b in range(in_blocks):
            msg_ref[b, leaf * 4 * half : (leaf + 1) * 4 * half, :] = out[
                :, b * block : (b + 1) * block
            ]


def field_kernel(
    idx_ref,
    rep_ref,
    sid_ref,
    own_ref,
    slot_ref,
    disp_ref,
    me_ref,
    prev_hbm,
    here_hbm,
    next_hbm,
    val_ref,
    shift_ref,
    trans_ref,
    *rest,
    n_samp,
    leaf_count,
    entries,
):
    outs = rest[:n_samp]
    msg_ref, top_ref, down_ref, acc_ref, sem = rest[n_samp:]
    step = pl.program_id(0)
    tile = val_ref.shape[0]
    block = val_ref.shape[2]
    leaves = top_ref.shape[0] - 1
    group = leaves // 3
    rows = 16 * leaf_count

    @pl.when(step == 0)
    def _():
        copies = [
            pltpu.make_async_copy(src, msg_ref.at[pl.ds(g * n_samp, n_samp)], sem.at[g])
            for g, src in enumerate((prev_hbm, here_hbm, next_hbm))
        ]
        for copy in copies:
            copy.start()
        acc_ref[...] = jnp.zeros_like(acc_ref)
        top_ref[leaves] = jnp.zeros(top_ref.shape[1:], F32)
        for copy in copies:
            copy.wait()

    def row(ref, index, b):
        return jnp.broadcast_to(ref[index, b : b + 1, :], (8, block))

    for b in range(tile):
        first, second = idx_ref[(step * tile + b) * 2], idx_ref[(step * tile + b) * 2 + 1]
        left = jnp.concatenate(
            [msg_ref[:, first, :rows, :], msg_ref[:, second, :rows, :]], axis=2
        ).reshape(leaves * 16, 2 * block)
        right = jnp.concatenate([val_ref[b, 0], val_ref[b, 1]], axis=1)
        moved = lax.dot_general(left, right, NT, preferred_element_type=F32)
        for s in range(leaves):
            real, imag = moved[s * 16 : s * 16 + 8], moved[s * 16 + 8 : s * 16 + 16]
            shift_real = row(shift_ref, 2 * sid_ref[s], b)
            shift_imag = row(shift_ref, 2 * sid_ref[s] + 1, b)
            up_real = real * shift_real - imag * shift_imag
            up_imag = real * shift_imag + imag * shift_real
            rep = rep_ref[s]
            fresh = rep == s
            top_ref[rep, 0, b] = jnp.where(fresh, 0.0, top_ref[rep, 0, b]) + up_real
            top_ref[rep, 1, b] = jnp.where(fresh, 0.0, top_ref[rep, 1, b]) + up_imag

    def target(leaf, carry):
        real = [jnp.zeros((8, block), F32) for _ in range(tile)]
        imag = [jnp.zeros((8, block), F32) for _ in range(tile)]
        for j in range(entries):
            slot, disp = slot_ref[leaf * entries + j], disp_ref[leaf * entries + j]
            for b in range(tile):
                coef_real = row(trans_ref, 2 * disp, b)
                coef_imag = row(trans_ref, 2 * disp + 1, b)
                src_real, src_imag = top_ref[slot, 0, b], top_ref[slot, 1, b]
                real[b] += coef_real * src_real - coef_imag * src_imag
                imag[b] += coef_real * src_imag + coef_imag * src_real
        sid = own_ref[leaf]
        for b in range(tile):
            shift_real = row(shift_ref, 2 * sid, b)
            shift_imag = row(shift_ref, 2 * sid + 1, b)
            down = jnp.concatenate(
                [
                    shift_real * real[b] + shift_imag * imag[b],
                    shift_real * imag[b] - shift_imag * real[b],
                ],
                axis=0,
            )
            down_ref[b, pl.ds(pl.multiple_of(leaf * 16, 16), 16), :] = down.astype(BF16)
        return carry

    lax.fori_loop(0, group, target, 0)

    for b in range(tile):
        first, second = idx_ref[(step * tile + b) * 2], idx_ref[(step * tile + b) * 2 + 1]
        right = jnp.concatenate([val_ref[b, 0], val_ref[b, 1]], axis=1)
        part = jnp.dot(down_ref[b], right, preferred_element_type=F32)
        acc_ref[first] += part[:, :block]
        acc_ref[second] += part[:, block:]

    @pl.when(step == pl.num_programs(0) - 1)
    def _():
        me = me_ref[0]
        for d, out in enumerate(outs):
            owner = lax.rem(me + d, n_samp)
            start = pl.multiple_of(owner * rows, rows)
            out[...] = acc_ref[:, pl.ds(start, rows), :].astype(BF16)


def near_kernel(src_ref, prev_hbm, here_hbm, next_hbm, near_hbm, out_ref, cur_ref, near_ref, sem):
    leaf_count, near = near_ref.shape[:2]
    n_samp = prev_hbm.shape[0]
    in_blocks = prev_hbm.shape[1]
    extra = cur_ref.shape[2]
    base = prev_hbm.shape[2] - extra
    copies = [
        pltpu.make_async_copy(
            src.at[:, :, pl.ds(base, extra), :], cur_ref.at[pl.ds(g * n_samp, n_samp)], sem.at[g]
        )
        for g, src in enumerate((prev_hbm, here_hbm, next_hbm))
    ] + [
        pltpu.make_async_copy(near_hbm.at[leaf], near_ref.at[leaf], sem.at[3 + leaf])
        for leaf in range(leaf_count)
    ]
    for copy in copies:
        copy.start()
    for copy in copies[:3]:
        copy.wait()
    for leaf in range(leaf_count):
        left = []
        right = []
        for n in range(near):
            src = src_ref[leaf * near + n]
            piece, inner = src // leaf_count, lax.rem(src, leaf_count)
            start = pl.multiple_of(inner // in_blocks * 16, 16)
            both = cur_ref[piece, lax.rem(inner, in_blocks), pl.ds(start, 16), :].astype(F32)
            real, imag = both[:4], both[4:8]
            left.append(both[:8].astype(BF16))
            left.append(jnp.concatenate([-imag, real], axis=0).astype(BF16))
        copies[3 + leaf].wait()
        for n in range(near):
            right += [near_ref[leaf, n, 0], near_ref[leaf, n, 1]]
        out_ref[leaf] = lax.dot_general(
            jnp.concatenate(left, axis=1),
            jnp.concatenate(right, axis=1),
            NT,
            preferred_element_type=F32,
        )


def receive_kernel(near_ref, rad_hbm, *rest, n_samp):
    far_refs = rest[:n_samp]
    out_ref, rad_ref, sem = rest[n_samp:]
    leaf_count = out_ref.shape[0]
    copies = [
        pltpu.make_async_copy(rad_hbm.at[leaf], rad_ref.at[leaf], sem.at[leaf])
        for leaf in range(leaf_count)
    ]
    for copy in copies:
        copy.start()
    far = far_refs[0][...].astype(F32)
    for ref in far_refs[1:]:
        far = far + ref[...].astype(F32)
    in_blocks = far.shape[0]
    unknowns = rad_ref.shape[4]
    depth = rad_ref.shape[1] * rad_ref.shape[2] * rad_ref.shape[3]
    for leaf in range(leaf_count):
        left = []
        for p in range(2):
            real = [far[b, leaf * 16 + p * 4 : leaf * 16 + p * 4 + 4] for b in range(in_blocks)]
            imag = [
                far[b, leaf * 16 + 8 + p * 4 : leaf * 16 + 12 + p * 4] for b in range(in_blocks)
            ]
            left += [jnp.concatenate(pair, axis=0) for pair in zip(real, imag)]
            left += [jnp.concatenate([i, -r], axis=0) for r, i in zip(real, imag)]
        wide = jnp.concatenate(left, axis=1).astype(BF16)
        copies[leaf].wait()
        right = rad_ref[leaf].reshape(depth, unknowns)
        out_ref[leaf] = near_ref[leaf] + jnp.dot(wide, right, preferred_element_type=F32)


def per_device(
    currents,
    radiation,
    near_blocks,
    near_src,
    leaf_parent,
    leaf_shift,
    shift_table,
    interp_idx,
    interp_val,
    top_src,
    top_disp,
    trans_table,
):
    n_samp = lax.axis_size("samp")
    n_box = lax.axis_size("box")
    group_index = lax.axis_index("box")
    me = lax.axis_index("samp")
    leaf_count, comps, unknowns = currents.shape
    group = leaf_parent.shape[0]
    top_count, entries = top_src.shape
    local_blocks, _, block, _ = interp_val.shape
    in_blocks = radiation.shape[3] // block
    near = near_src.shape[1]
    leaves = 3 * group
    rows = 16 * leaf_count
    extra = 16 * -(-leaf_count // in_blocks)
    tile = min(8, local_blocks)
    steps = local_blocks // tile

    parent_local = leaf_parent - group_index * top_count
    meta = jnp.zeros((8, block), F32)
    meta = meta.at[0, :group].set(parent_local.astype(F32))
    meta = meta.at[1, :group].set(leaf_shift.astype(F32))

    message = pl.pallas_call(
        radiate_kernel,
        out_shape=jax.ShapeDtypeStruct((in_blocks, rows + extra, block), BF16),
        in_specs=[VMEM, VMEM, ANY],
        out_specs=VMEM,
        scratch_shapes=[
            pltpu.VMEM(radiation.shape, BF16),
            pltpu.SemaphoreType.DMA((leaf_count,)),
        ],
        compiler_params=params(),
        name="radiate",
    )(currents, meta, radiation)
    here = lax.all_gather(message, "samp", axis=0)
    before = lax.ppermute(here, "box", [(i, i + 1) for i in range(n_box - 1)])
    after = lax.ppermute(here, "box", [(i + 1, i) for i in range(n_box - 1)])

    def numbers(piece):
        found = piece[0, 0, rows + 8 : rows + 10, :group].astype(jnp.int32)
        return found[0], found[1]

    parent_before, shift_before = numbers(before)
    parent_after, shift_after = numbers(after)
    parents = jnp.concatenate(
        [parent_before, parent_local + top_count, parent_after + 2 * top_count]
    )
    shifts = jnp.concatenate([shift_before, leaf_shift, shift_after])
    order = jnp.arange(leaves, dtype=jnp.int32)
    rep = jnp.min(
        jnp.where(parents[:, None] == parents[None, :], order[None, :], leaves), axis=1
    )
    chosen = (parent_local[:, None] == jnp.arange(top_count)[None, :])[:, :, None]
    sources = jnp.sum(jnp.where(chosen, top_src[None], 0), axis=1)
    sources = sources - (group_index - 1) * top_count
    displace = jnp.sum(jnp.where(chosen, top_disp[None], 0), axis=1)
    slots = jnp.min(
        jnp.where(sources[:, :, None] == parents[None, None, :], order[None, None, :], leaves),
        axis=2,
    )
    shift_rows = shift_table.astype(F32).reshape(-1, local_blocks, block)
    trans_rows = trans_table.astype(F32).reshape(-1, local_blocks, block)

    fars = pl.pallas_call(
        functools.partial(
            field_kernel, n_samp=n_samp, leaf_count=leaf_count, entries=entries
        ),
        out_shape=[jax.ShapeDtypeStruct((in_blocks, rows, block), BF16)] * n_samp,
        grid=(steps,),
        in_specs=[SMEM] * 7
        + [ANY] * 3
        + [
            pl.BlockSpec((tile, 2, block, block), lambda t: (t, 0, 0, 0)),
            pl.BlockSpec((shift_rows.shape[0], tile, block), lambda t: (0, t, 0)),
            pl.BlockSpec((trans_rows.shape[0], tile, block), lambda t: (0, t, 0)),
        ],
        out_specs=[pl.BlockSpec((in_blocks, rows, block), lambda t: (0, 0, 0))] * n_samp,
        scratch_shapes=[
            pltpu.VMEM((3 * n_samp,) + message.shape, BF16),
            pltpu.VMEM((leaves + 1, 2, tile, 8, block), F32),
            pltpu.VMEM((tile, group * 16, block), BF16),
            pltpu.VMEM((in_blocks, group * 16, block), F32),
            pltpu.SemaphoreType.DMA((3,)),
        ],
        compiler_params=params(),
        name="field",
    )(
        interp_idx.reshape(-1),
        rep,
        shifts,
        leaf_shift,
        slots.reshape(-1),
        displace.reshape(-1),
        me[None],
        before,
        here,
        after,
        interp_val,
        shift_rows,
        trans_rows,
    )
    received = [fars[0]] + [
        lax.ppermute(fars[d], "samp", [(i, (i + d) % n_samp) for i in range(n_samp)])
        for d in range(1, n_samp)
    ]
    near_out = pl.pallas_call(
        near_kernel,
        out_shape=jax.ShapeDtypeStruct((leaf_count, comps, unknowns), F32),
        in_specs=[SMEM] + [ANY] * 4,
        out_specs=VMEM,
        scratch_shapes=[
            pltpu.VMEM((3 * n_samp, in_blocks, extra, block), BF16),
            pltpu.VMEM(near_blocks.shape, BF16),
            pltpu.SemaphoreType.DMA((3 + leaf_count,)),
        ],
        compiler_params=params(),
        name="near",
    )(
        (near_src - (group_index - 1) * group).reshape(-1),
        before,
        here,
        after,
        near_blocks,
    )
    return pl.pallas_call(
        functools.partial(receive_kernel, n_samp=n_samp),
        out_shape=jax.ShapeDtypeStruct((leaf_count, comps, unknowns), F32),
        in_specs=[VMEM, ANY] + [VMEM] * n_samp,
        out_specs=VMEM,
        scratch_shapes=[
            pltpu.VMEM(radiation.shape, BF16),
            pltpu.SemaphoreType.DMA((leaf_count,)),
        ],
        compiler_params=params(),
        name="receive",
    )(near_out, radiation, *received)


def solution(mesh):
    placed = (
        P(("box", "samp"), None, None),
        P(("box", "samp"), None, None, None, None),
        P(("box", "samp"), None, None, None, None),
        P(("box", "samp"), None),
        P("box"),
        P("box"),
        P(None, None, "samp"),
        P("samp", None),
        P("samp", None, None, None),
        P("box", None),
        P("box", None),
        P(None, None, "samp"),
    )
    return jax.shard_map(
        per_device,
        mesh=mesh,
        in_specs=placed,
        out_specs=P(("box", "samp"), None, None),
        check_vma=False,
    )
```

time: 376 us -> 48.1 us (0.13)
  other arithmetic: 184 us -> 4.67 us
  local copies, waits for them, and re-layouts: 85.7 us -> 9.82 us
  waiting for transfers between devices: 46.2 us -> 4.43 us
  matrix products: 31.7 us -> 0 us
  Pallas kernels: 0 us -> 20.3 us
  between operations: 13.7 us -> 0.16 us
  starting transfers between devices: 10.1 us -> 6.1 us
    add x16 -> x1, other arithmetic: 102 us -> 0.69 us  [per_device(): parent_local + top_count]
    gather x18 -> x0, local copies, waits for them, and re-layouts: 71 us -> none  [the longest x16 68.1 us: add_entry(): jnp.take(padded, top_src[:, entry] - base_index, axis=0).astype(jnp.float32)]
    sub x18 -> x2, other arithmetic: 44.5 us -> 0.82 us  [the longest x1 0.82 us: per_device(): near_src - (group_index - 1) * group]
    ppermute x4 -> x3, waiting for transfers between devices: 40.9 us -> 4.43 us  [the longest x1 4.42 us: per_device(): after = lax.ppermute(here, 'box', [(i + 1, i) for i in range(n_box - 1)])]
    convert_element_type x17 -> x2, other arithmetic: 33.3 us -> 0.69 us  [numbers(): found = piece[0, 0, rows + 8:rows + 10, :group].astype(jnp.int32)]
    dot_general x34 -> x0, matrix products: 31.7 us -> none  [the longest x32 25.4 us: contract(): jnp.einsum(form, first_op, second_op, preferred_element_type=jnp.float32)]
    pallas_call x0 -> x4, Pallas kernels: none -> 20.3 us  [the longest x1 14.6 us: per_device(): pl.pallas_call(functools.partial(field_kernel, n_samp=n_samp, leaf_count=...]
    reduce_scatter x1 -> x0, waiting for transfers between devices: 5.25 us -> none  [per_device(): lax.psum_scatter(folded.reshape(leaf_count * lax.axis_size('samp'), comps...]
  transfers between devices with their start and end apart: 5 -> 3, of which waited for: 4 -> 1; matrix products, arithmetic and copies ran while one was open for 1% -> 9% of each run, Pallas kernels for 0% -> 6%
where the time goes in v1:
time: 48.1 us; the launch traced here: 47.5 us
  Pallas kernels  20.3 us (42%)
  local copies, waits for them, and re-layouts  9.82 us (20%)
  starting transfers between devices  6.1 us (13%)
  other arithmetic  4.67 us (10%)
  waiting for transfers between devices  4.43 us (9%)
  blocking collectives  2.02 us (4%)
    pallas_call x1, Pallas kernels, per_device(): pl.pallas_call(functools.partial(field_kernel, n_samp=n_samp, leaf_count=...  14.6 us
    unnamed x25, local copies, waits for them, and re-layouts  6.26 us
    ppermute x1, starting transfers between devices, per_device(): before = lax.ppermute(here, 'box', [(i, i + 1) for i in range(n_box - 1)])  4.74 us
    ppermute x1, waiting for transfers between devices, per_device(): after = lax.ppermute(here, 'box', [(i + 1, i) for i in range(n_box - 1)])  4.42 us
    pallas_call x1, Pallas kernels, per_device(): pl.pallas_call(near_kernel, out_shape=jax.ShapeDtypeStruct((leaf_count, c...  2.97 us
    all_gather x1, blocking collectives, per_device(): here = lax.all_gather(message, 'samp', axis=0)  2.02 us
    reshape x1, local copies, waits for them, and re-layouts, per_device(): shift_rows = shift_table.astype(F32).reshape(-1, local_blocks, block)  1.69 us
    pallas_call x1, Pallas kernels, per_device(): pl.pallas_call(functools.partial(receive_kernel, n_samp=n_samp), out_shap...  1.56 us
  transfers between devices with their start and end apart: 3, of which 1 were waited for; matrix products, arithmetic and copies ran while one was open for 9% of the time, Pallas kernels for 6%

profile of v1, /device:TPU:0, one launch (start us, length us, event | category | flops | bytes accessed | tf_op | source)
XLA Modules:
  0.0 47.5 jit_solution(3883876442493641084)
XLA Ops:
  0.0 0.7 %broadcast_add_fusion = (s32[8]{0:T(128)S(1)}, s32[8]{0:T(128)S(1)}) fusion(s32[8]{0:T(128)} %param.20, s32[]{:T(128)S(6)} %mul.10), kind=kLoop, calls=%fused_computation.17 | loop fusion | flops 16 | bytes 100 | tf_op jit(solution)/shard_map/add | solution.py:301
  0.7 0.7 %convert_bitcast_fusion = f32[1,8]{1,0:T(1,128)S(1)} fusion(s32[8]{0:T(128)} %own_ref.1), kind=kLoop, calls=%fused_computation.15 | loop fusion | flops 8 | bytes 64 | tf_op jit(solution)/shard_map/reshape.43
  1.4 0.1 scatter.9.meta_ref
  1.5 1.6 %copy-done = bf16[4,2,2,512,128]{4,3,2,1,0:T(8,128)(2,1)S(1)} copy-done((bf16[4,2,2,512,128]{4,3,2,1,0:T(8,128)(2,1)S(1)}, bf16[4,2,2,512,128]{4,3,2,1,0:T(8,128)(2,1)}, u32[]{:S(2)}) %copy-start) | copy-done | bytes 2097176
  3.1 0.7 %copy-done.5 = bf16[4,8,128]{2,1,0:T(8,128)(2,1)S(1)} copy-done((bf16[4,8,128]{2,1,0:T(8,128)(2,1)S(1)}, bf16[4,8,128]{2,1,0:T(8,128)(2,1)}, u32[]{:S(2)}) %copy-start.5) | copy-done | bytes 8216
  3.8 1.2 %radiate.1 = bf16[4,80,128]{2,1,0:T(8,128)(2,1)S(1)} custom-call(bf16[4,8,128]{2,1,0:T(8,128)(2,1)S(1)} %copy-done.5, f32[8,128]{1,0:T(8,128)S(1)} %scatter.9.meta_ref, bf16[4,2,2,512,128]{4,3,2,1,0:T(8,128)(2,1)S(1)} %copy-done), custom_call_target="tpu_custom_call" | custom-call | tf_op jit(solution)/shard_map/radiate/pallas_call | solution.py:278
  5.0 2.0 %all-gather = bf16[8,80,128]{2,1,0:T(8,128)(2,1)S(1)} all-gather(bf16[4,80,128]{2,1,0:T(8,128)(2,1)S(1)} %radiate.1), channel_id=2, replica_groups=mesh['box'=16,'samp'=2] {'samp'}, dimensions={0}, use_global_device_ids=true | all-gather | bytes 245760 | tf_op jit(solution)/shard_map/all_gather | solution.py:290
  7.0 4.7 %collective-permute-start = (bf16[2,4,80,128]{3,2,1,0:T(8,128)(2,1)S(1)}, bf16[2,4,80,128]{3,2,1,0:T(8,128)(2,1)S(1)}, u32[]{:S(2)}, u32[]{:S(2)}) collective-permute-start(bf16[2,4,80,128]{3,2,1,0:T(8,128)(2,1)S(1)} %bitcast.14), channel_id=1, source_target_pairs={{0,2},{2,4},{4,6},{6,8},{8,10},{10,12},{12,14},{14,16},{16,18},{18... | collective-permute-start | bytes 491528 | tf_op jit(solution)/shard_map/ppermute | solution.py:291
  11.8 1.3 %collective-permute-start.1 = (bf16[2,4,80,128]{3,2,1,0:T(8,128)(2,1)S(1)}, bf16[2,4,80,128]{3,2,1,0:T(8,128)(2,1)}, u32[]{:S(2)}, u32[]{:S(2)}) collective-permute-start(bf16[2,4,80,128]{3,2,1,0:T(8,128)(2,1)S(1)} %bitcast.15), channel_id=1, source_target_pairs={{2,0},{4,2},{6,4},{8,6},{10,8},{12,10},{14,12},{16,14},{18,16},{20... | collective-permute-start | bytes 491528 | tf_op jit(solution)/shard_map/ppermute | solution.py:292
  13.1 0.1 iota_compare_fusion
  13.2 0.1 select_reduce_fusion
  13.3 0.1 reshape.129.disp_ref
  13.3 1.4 %reshape.137.trans_ref = f32[64,32,128]{2,1,0:T(8,128)S(1)} reshape(bf16[32,2,4096]{2,1,0:T(2,128)(2,1)} %param.27) | data formatting | bytes 1572864 | tf_op jit(solution)/shard_map/reshape | solution.py:317
  14.7 1.7 %reshape.135.shift_ref = f32[16,32,128]{2,1,0:T(8,128)} reshape(bf16[8,2,4096]{2,1,0:T(2,128)(2,1)} %param.22) | data formatting | bytes 393216 | tf_op jit(solution)/shard_map/reshape | solution.py:316
  16.4 0.1 copy.16
  16.5 0.1 reshape.127.idx_ref
  16.7 4.4 %collective-permute-done.1.next_hbm = bf16[2,4,80,128]{3,2,1,0:T(8,128)(2,1)} collective-permute-done((bf16[2,4,80,128]{3,2,1,0:T(8,128)(2,1)S(1)}, bf16[2,4,80,128]{3,2,1,0:T(8,128)(2,1)}, u32[]{:S(2)}, u32[]{:S(2)}) %collective-permute-start.1) | collective-permute-done | bytes 163872 | tf_op jit(solution)/shard_map/ppermute | solution.py:292
  21.1 0.7 %slice_convert_fusion = s32[1,1,2,8]{3,2,1,0:T(2,128)S(1)} fusion(bf16[2,4,80,128]{3,2,1,0:T(8,128)(2,1)} %collective-permute-done.1.next_hbm), kind=kLoop, calls=%fused_computation.7 | loop fusion | flops 16 | bytes 96 | tf_op jit(solution)/shard_map/convert_element_type | solution.py:295
  21.8 0.6 %pad_add_fusion = (s32[24]{0:T(128)S(1)}, s32[24]{0:T(128)}) fusion(s32[8]{0:T(128)S(1)} %get-tuple-element.40, s32[8]{0:T(128)S(1)} %get-tuple-element.35, s32[8]{0:T(128)S(1)} %get-tuple-element.38, s32[8]{0:T(128)S(1)} %get-tuple-element.39, s32[8]{0:T(128)S(1)} %copy-done.6, s32[8]{0:T(128)S(1)} %get-tuple-element.37), kind=kLoop, calls=%fused_computation.9 | loop fusion | flops 96 | bytes 384 | tf_op jit(solution)/shard_map/concatenate | solution.py:300
  22.4 0.8 %select_reduce_fusion.3.rep_ref = s32[24]{0:T(128)} fusion(s32[24]{0:T(128)S(1)} %get-tuple-element.41), kind=kLoop, calls=%fused_computation.3 | loop fusion | flops 1704 | bytes 192 | tf_op jit(solution)/shard_map/reduce_min | solution.py:305
  23.1 0.3 select_reduce_fusion.1
  23.4 0.1 reshape.128.slot_ref
  23.5 1.0 %copy-done.4 = f32[16,32,128]{2,1,0:T(8,128)S(1)} copy-done((f32[16,32,128]{2,1,0:T(8,128)S(1)}, f32[16,32,128]{2,1,0:T(8,128)}, u32[]{:S(2)}) %copy-start.4) | copy-done | bytes 262168
  24.5 0.7 %copy-done.7 = s32[24]{0:T(128)S(1)} copy-done((s32[24]{0:T(128)S(1)}, s32[24]{0:T(128)}, u32[]{:S(2)}) %copy-start.7) | copy-done | bytes 120
  25.1 0.7 %copy-done.8 = s32[24]{0:T(128)S(1)} copy-done((s32[24]{0:T(128)S(1)}, s32[24]{0:T(128)}, u32[]{:S(2)}) %copy-start.8) | copy-done | bytes 120
  25.8 14.6 %field.1 = (bf16[4,64,128]{2,1,0:T(8,128)(2,1)S(1)}, bf16[4,64,128]{2,1,0:T(8,128)(2,1)}) custom-call(s32[64]{0:T(128)S(1)} %reshape.127.idx_ref, s32[24]{0:T(128)S(1)} %copy-done.8, s32[24]{0:T(128)S(1)} %copy-done.7, s32[8]{0:T(128)S(1)} %copy-done.6, s32[128]{0:T(128)S(1)} %reshape.128.slot_ref, s32[128]{0:T(128)S(1)} %reshape.129.disp_ref, ...), custom_call_target="tpu_custom_call" | custom-call | tf_op jit(solution)/shard_map/field/pallas_call | solution.py:319
  40.4 0.1 collective-permute-start.2
  40.5 0.8 %broadcast_subtract_fusion.1 = s32[4,8]{1,0:T(4,128)S(1)} fusion(s32[4,8]{1,0:T(4,128)} %param.19, s32[]{:T(128)S(6)} %mul.9), kind=kLoop, calls=%fused_computation.6 | loop fusion | flops 32 | bytes 260 | tf_op jit(solution)/shard_map/sub | solution.py:374
  41.3 0.1 reshape.124.src_ref
  41.4 1.6 %copy-done.3 = bf16[4,8,2,128,128]{4,3,2,1,0:T(8,128)(2,1)S(1)} copy-done((bf16[4,8,2,128,128]{4,3,2,1,0:T(8,128)(2,1)S(1)}, bf16[4,8,2,128,128]{4,3,2,1,0:T(8,128)(2,1)}, u32[]{:S(2)}) %copy-start.3) | copy-done | bytes 2097176
  43.0 3.0 %near.1.near_ref = f32[4,8,128]{2,1,0:T(8,128)S(1)} custom-call(s32[32]{0:T(128)S(1)} %reshape.124.src_ref, bf16[2,4,80,128]{3,2,1,0:T(8,128)(2,1)S(1)} %collective-permute-done.prev_hbm, bf16[2,4,80,128]{3,2,1,0:T(8,128)(2,1)S(1)} %bitcast.17, bf16[2,4,80,128]{3,2,1,0:T(8,128)(2,1)} %collective-permute-done.1.next_hbm, ...), custom_call_target="tpu_custom_call" | custom-call | tf_op jit(solution)/shard_map/near/pallas_call | solution.py:361
  46.0 1.6 %receive.1 = f32[4,8,128]{2,1,0:T(8,128)} custom-call(f32[4,8,128]{2,1,0:T(8,128)S(1)} %near.1.near_ref, bf16[4,2,2,512,128]{4,3,2,1,0:T(8,128)(2,1)S(1)} %copy-done.1, bf16[4,64,128]{2,1,0:T(8,128)(2,1)S(1)} %get-tuple-element.31.rest_0_, bf16[4,64,128]{2,1,0:T(8,128)(2,1)S(1)} %collective-permute-done.2.rest_1_), custom_call_target="tpu_custom_call" | custom-call | tf_op jit(solution)/shard_map/receive/pallas_call | solution.py:380
  (26 shorter events, 0.1 us)
Async XLA Ops:
  0.0 13.1 %copy-start.10 = (s32[16,16]{1,0:T(8,128)S(1)}, s32[16,16]{1,0:T(8,128)}, u32[]{:S(2)}) copy-start(s32[16,16]{1,0:T(8,128)} %param.25) | copy-start | bytes 3076
  0.0 13.1 %copy-start.9 = (s32[16,16]{1,0:T(8,128)S(1)}, s32[16,16]{1,0:T(8,128)}, u32[]{:S(2)}) copy-start(s32[16,16]{1,0:T(8,128)} %param.26) | copy-start | bytes 3076
  1.5 1.6 %copy-start = (bf16[4,2,2,512,128]{4,3,2,1,0:T(8,128)(2,1)S(1)}, bf16[4,2,2,512,128]{4,3,2,1,0:T(8,128)(2,1)}, u32[]{:S(2)}) copy-start(bf16[4,2,2,512,128]{4,3,2,1,0:T(8,128)(2,1)} %rad_hbm.3) | copy-start | bytes 6291460
  3.1 0.7 %copy-start.5 = (bf16[4,8,128]{2,1,0:T(8,128)(2,1)S(1)}, bf16[4,8,128]{2,1,0:T(8,128)(2,1)}, u32[]{:S(2)}) copy-start(bf16[4,8,128]{2,1,0:T(8,128)(2,1)} %cur_ref.1) | copy-start | bytes 24580
  3.8 12.6 %copy-start.11 = (s32[32,2]{0,1:T(2,128)S(1)}, s32[32,2]{0,1:T(2,128)}, u32[]{:S(2)}) copy-start(s32[32,2]{0,1:T(2,128)} %param.23) | copy-start | bytes 772
  3.8 18.0 %copy-start.6 = (s32[8]{0:T(128)S(1)}, s32[8]{0:T(128)}, u32[]{:S(2)}) copy-start(s32[8]{0:T(128)} %own_ref.1) | copy-start | bytes 100
  3.8 19.7 %copy-start.2 = (bf16[32,2,128,128]{3,2,1,0:T(8,128)(2,1)S(1)}, bf16[32,2,128,128]{3,2,1,0:T(8,128)(2,1)}, u32[]{:S(2)}) copy-start(bf16[32,2,128,128]{3,2,1,0:T(8,128)(2,1)} %val_ref.1) | copy-start | bytes 6291460
  7.0 9.6 %collective-permute-start = (bf16[2,4,80,128]{3,2,1,0:T(8,128)(2,1)S(1)}, bf16[2,4,80,128]{3,2,1,0:T(8,128)(2,1)S(1)}, u32[]{:S(2)}, u32[]{:S(2)}) collective-permute-start(bf16[2,4,80,128]{3,2,1,0:T(8,128)(2,1)S(1)} %bitcast.14), channel_id=1, source_target_pairs={{0,2},{2,4},{4,6},{6,8},{8,10},{10,12},{12,14},{14,16},{16,18},{18... | collective-permute-start | bytes 491528 | tf_op jit(solution)/shard_map/ppermute | solution.py:291
  11.8 9.3 %collective-permute-start.1 = (bf16[2,4,80,128]{3,2,1,0:T(8,128)(2,1)S(1)}, bf16[2,4,80,128]{3,2,1,0:T(8,128)(2,1)}, u32[]{:S(2)}, u32[]{:S(2)}) collective-permute-start(bf16[2,4,80,128]{3,2,1,0:T(8,128)(2,1)S(1)} %bitcast.15), channel_id=1, source_target_pairs={{2,0},{4,2},{6,4},{8,6},{10,8},{12,10},{14,12},{16,14},{18,16},{20... | collective-permute-start | bytes 491528 | tf_op jit(solution)/shard_map/ppermute | solution.py:292
  23.5 1.0 %copy-start.4 = (f32[16,32,128]{2,1,0:T(8,128)S(1)}, f32[16,32,128]{2,1,0:T(8,128)}, u32[]{:S(2)}) copy-start(f32[16,32,128]{2,1,0:T(8,128)} %reshape.135.shift_ref) | copy-start | bytes 786436
  24.5 0.7 %copy-start.7 = (s32[24]{0:T(128)S(1)}, s32[24]{0:T(128)}, u32[]{:S(2)}) copy-start(s32[24]{0:T(128)} %get-tuple-element.42.sid_ref) | copy-start | bytes 292
  25.1 0.7 %copy-start.8 = (s32[24]{0:T(128)S(1)}, s32[24]{0:T(128)}, u32[]{:S(2)}) copy-start(s32[24]{0:T(128)} %select_reduce_fusion.3.rep_ref) | copy-start | bytes 292
  40.4 5.6 %copy-start.1 = (bf16[4,2,2,512,128]{4,3,2,1,0:T(8,128)(2,1)S(1)}, bf16[4,2,2,512,128]{4,3,2,1,0:T(8,128)(2,1)}, u32[]{:S(2)}) copy-start(bf16[4,2,2,512,128]{4,3,2,1,0:T(8,128)(2,1)} %rad_hbm.3) | copy-start | bytes 6291460
  40.4 5.6 %collective-permute-start.2 = (bf16[4,64,128]{2,1,0:T(8,128)(2,1)}, bf16[4,64,128]{2,1,0:T(8,128)(2,1)S(1)}, u32[]{:S(2)}, u32[]{:S(2)}) collective-permute-start(bf16[4,64,128]{2,1,0:T(8,128)(2,1)} %get-tuple-element.32), channel_id=1, source_target_pairs={{0,1},{1,0},{2,3},{3,2},{4,5},{5,4},{6,7},{7,6},{8,9},{9,8},{10,11... | collective-permute-start | bytes 196616 | tf_op jit(solution)/shard_map/ppermute | solution.py:358
  41.4 1.6 %copy-start.3 = (bf16[4,8,2,128,128]{4,3,2,1,0:T(8,128)(2,1)S(1)}, bf16[4,8,2,128,128]{4,3,2,1,0:T(8,128)(2,1)}, u32[]{:S(2)}) copy-start(bf16[4,8,2,128,128]{4,3,2,1,0:T(8,128)(2,1)} %near_hbm.1) | copy-start | bytes 6291460
